TPU v7x, 32 devices: a whole 2x2x4 slice. The times are simulated.
32 devices in a mesh: groups: 2 (over y), lat: 16 (over z, x, core).
Axes of the slice: x: 2, y: 2, z: 4, core: 2. Of those that a mesh axis runs over, the one named last changes fastest.
Arguments:
- acts: bfloat16 [32768, 128], P(('groups', 'lat')), parts along dimension 0, may hold values from -6 to 6
- mask: int32 [3072, 128], P(('groups', 'lat')), parts along dimension 0, may hold values from 0 to 3
- enc_weight: bfloat16 [3072, 16384], P(('groups', 'lat')), parts along dimension 0, may hold values from -0.046875 to 0.046875
- enc_bias: float32 [3072], P(('groups', 'lat')), parts along dimension 0, may hold values from -3 to 3
- threshold: float32 [3072], P(('groups', 'lat')), parts along dimension 0, may hold values from 0.05 to 0.5
- dec_weight: bfloat16 [3072, 16384], P(('groups', 'lat')), parts along dimension 0, may hold values from -0.21875 to 0.21875
- dec_bias: float32 [32768], P(('groups', 'lat')), parts along dimension 0, may hold values from -3 to 3
Outputs:
- grad_enc: bfloat16 [3072, 16384], P(('groups', 'lat')), parts along dimension 0
- grad_enc_bias: float32 [3072], P(('groups', 'lat')), parts along dimension 0
- grad_theta: float32 [3072], P(('groups', 'lat')), parts along dimension 0
- grad_dec: bfloat16 [3072, 16384], P(('groups', 'lat')), parts along dimension 0
- grad_dec_bias: float32 [32768], P(('groups', 'lat')), parts along dimension 0
There are 2 independent parts, one for each index of `groups`. A program takes and returns all parts, laid end to end along the dimension named above; each array names one. Nothing has to cross between parts.
Inputs may be any that keep to these rules, and one draw needn't show every extreme that they name: mask % 2 is 1 where a latent's JumpReLU gate is open for a token; mask // 2 is 1 where the token lies inside that latent's threshold window.
All inputs are finite; a program needn't handle non-finite values.
Results may differ from a plain program's by a relative error of at most 0.0058.
Values may be sent and summed in bfloat16 or wider, within the bound.
A program may use at most 64 MiB of HBM per device.

v0:
```python
import math

import jax
import jax.numpy as jnp
from jax import lax
from jax.sharding import PartitionSpec as P

sparsity_coef = 0.1
spread = 0.1
norm_eps = 1e-06


def per_device(acts, mask, enc_weight, enc_bias, threshold, dec_weight, dec_bias):
    latents, tokens = mask.shape
    total_width = dec_weight.shape[1]
    half_width = total_width // 2
    scale = 1.0 / math.sqrt(tokens)
    tokdims = (((1,), (1,)), ((), ()))
    firstdims = (((0,), (0,)), ((), ()))
    gathered = lax.all_gather(acts, "lat", axis=0, tiled=True)
    pre = jnp.dot(enc_weight, gathered, preferred_element_type=jnp.float32)
    pre = pre + enc_bias[:, None]
    active = (mask % 2).astype(jnp.float32)
    window = (mask // 2).astype(jnp.float32)
    feats = (active * pre).astype(jnp.bfloat16)
    all_feats = lax.all_gather(feats, "lat", axis=0, tiled=True)
    own_columns = lax.all_to_all(dec_weight, "lat", split_axis=1, concat_axis=0, tiled=True)
    recon = lax.dot_general(own_columns, all_feats, firstdims, preferred_element_type=jnp.float32)
    error = (recon + dec_bias[:, None] - acts.astype(jnp.float32)).astype(jnp.bfloat16)
    all_errors = lax.all_gather(error, "lat", axis=0, tiled=True)
    grec = jnp.dot(dec_weight, all_errors, preferred_element_type=jnp.float32)
    cross = lax.dot_general(feats, all_errors, tokdims, preferred_element_type=jnp.float32)
    gpre = (active * grec).astype(jnp.bfloat16)
    enc_grad = lax.dot_general(gpre, gathered, tokdims, preferred_element_type=jnp.float32)
    grad_enc = (scale * enc_grad).astype(jnp.bfloat16)
    grad_enc_bias = scale * jnp.sum(gpre.astype(jnp.float32), axis=1)
    base_part = dec_weight[:, :half_width].astype(jnp.float32)
    adjusted_part = dec_weight[:, half_width:].astype(jnp.float32)
    norm_base = jnp.sqrt(jnp.sum(base_part * base_part, axis=1) + norm_eps)
    norm_adjusted = jnp.sqrt(jnp.sum(adjusted_part * adjusted_part, axis=1) + norm_eps)
    weight_sum = norm_base + norm_adjusted
    grad_theta = -(scale / spread) * jnp.sum(
        window * (threshold[:, None] * grec + sparsity_coef * weight_sum[:, None]), axis=1
    )
    counts = jnp.sum(active, axis=1)
    unit = jnp.concatenate(
        [base_part / norm_base[:, None], adjusted_part / norm_adjusted[:, None]], axis=1
    )
    grad_dec = (scale * (cross + sparsity_coef * counts[:, None] * unit)).astype(jnp.bfloat16)
    grad_dec_bias = scale * jnp.sum(error.astype(jnp.float32), axis=1)
    return (grad_enc, grad_enc_bias, grad_theta, grad_dec, grad_dec_bias)


def solution(mesh):
    in_specs = (
        P(("groups", "lat"), None),
        P(("groups", "lat"), None),
        P(("groups", "lat"), None),
        P(("groups", "lat")),
        P(("groups", "lat")),
        P(("groups", "lat"), None),
        P(("groups", "lat")),
    )
    out_specs = (
        P(("groups", "lat"), None),
        P(("groups", "lat")),
        P(("groups", "lat")),
        P(("groups", "lat"), None),
        P(("groups", "lat")),
    )
    return jax.shard_map(
        per_device, mesh=mesh, in_specs=in_specs, out_specs=out_specs, check_vma=False
    )
```

profile of v0, /device:TPU:0, one launch (start us, length us, event | category | flops | bytes accessed | tf_op | source)
XLA Modules:
  0.0 202.6 jit_solution(12665712662746609814)
XLA Ops:
  7.2 0.0 copy-start
  7.2 0.0 all-gather.3.cloned.1.call-start
  7.2 0.7 all-gather.3.cloned.1.call-update
  7.9 4.2 %copy.20 = bf16[12,16,8,1024]{3,2,0,1:T(8,128)(2,1)} copy(bf16[12,16,8,1024]{3,2,1,0:T(8,128)(2,1)} %bitcast.25) | data formatting | bytes 6291456 | tf_op jit(solution)/shard_map/all_to_all | solution.py:27
  12.1 7.5 %all-to-all-start = ((bf16[96,16,1024]{2,0,1:T(8,128)(2,1)}), bf16[96,16,1024]{2,0,1:T(8,128)(2,1)}, u32[]{:S(2)}, u32[]{:S(2)}) async-start(bf16[96,16,1024]{2,0,1:T(8,128)(2,1)} %bitcast.26), calls=%async_computation | async-start | bytes 6291456 | tf_op jit(solution)/shard_map/all_to_all | solution.py:27
  19.7 0.0 all-gather.5.cloned.1.call-start
  19.7 0.9 copy.17
  20.6 80.6 %all-gather.3.cloned.1.call-done = bf16[16384,128]{1,0:T(8,128)(2,1)} async-done(((bf16[1024,128]{1,0:T(8,128)(2,1)}), bf16[16384,128]{1,0:T(8,128)(2,1)}) %all-gather.3.cloned.1.call-update) | async-done | bytes 4194320 | tf_op jit(solution)/shard_map/all_gather | solution.py:20
  101.2 3.2 %fusion.9 = bf16[96,128]{1,0:T(8,128)(2,1)S(1)} fusion(bf16[96,16384]{1,0:T(8,128)(2,1)S(1)} %copy-done, bf16[16384,128]{1,0:T(8,128)(2,1)} %all-gather.3.cloned.1.call-done, f32[96]{0:T(128)S(1)} %copy-done.12, s32[96,128]{1,0:T(8,128)S(1)} %copy-done.9), kind=kOutput, calls=%fused_computation.20 | convolution fusion | flops 402837504 | bytes 7414144 | tf_op jit(solution)/shard_map/dot_general | solution.py:21
  104.3 0.6 copy-done.7
  104.9 26.0 %all_gather.10 = bf16[1536,128]{1,0:T(8,128)(2,1)S(1)} all-gather(bf16[96,128]{1,0:T(8,128)(2,1)S(1)} %fusion.9), channel_id=1, replica_groups=mesh['groups'=2,'lat'=16] {'lat'}, dimensions={0}, use_global_device_ids=true | all-gather | bytes 417792 | tf_op jit(solution)/shard_map/all_gather | solution.py:26
  131.0 3.2 %convert_reduce_fusion = (f32[1024]{0:T(1024)S(1)}, bf16[1024,128]{0,1:T(8,128)(2,1)}) fusion(bf16[1024,128]{0,1:T(8,128)(2,1)} %copy.17, f32[1024]{0:T(1024)S(1)} %copy-done.11, bf16[1536,128]{1,0:T(8,128)(2,1)S(1)} %all_gather.10, bf16[1536,1024]{1,0:T(8,128)(2,1)} %bitcast.1), kind=kOutput, calls=%fused_computation.21 | convolution fusion | flops 403438592 | bytes 4071424 | tf_op jit(solution)/shard_map/dot_general | solution.py:28
  134.2 0.0 all-gather.5.cloned.1.call-update
  134.2 2.7 %fusion.4 = (f32[96]{0:T(128)S(1)}, f32[96]{0:T(128)S(1)}) fusion(bf16[96,16384]{1,0:T(8,128)(2,1)} %param.12), kind=kLoop, calls=%fused_computation.11 | loop fusion | flops 4718400 | bytes 3146496 | tf_op jit(solution)/shard_map/reduce_sum | solution.py:40
  137.0 0.1 copy-done.1
  137.1 3.5 %convert_divide_fusion.1 = (f32[96,8192]{1,0:T(8,128)}, f32[96,8192]{1,0:T(8,128)}) fusion(f32[96]{0:T(128)S(1)} %get-tuple-element.15, bf16[96,16384]{1,0:T(8,128)(2,1)S(1)} %copy-done.1, f32[96]{0:T(128)S(1)} %get-tuple-element.17), kind=kLoop, calls=%fused_computation.8 | loop fusion | flops 3145728 | bytes 9437952 | tf_op jit(solution)/shard_map/div | solution.py:47
  140.6 0.6 broadcast_multiply_fusion
  141.1 41.1 %all-gather.5.cloned.1.call-done = bf16[16384,128]{0,1:T(8,128)(2,1)} async-done(((bf16[1024,128]{0,1:T(8,128)(2,1)}), bf16[16384,128]{0,1:T(8,128)(2,1)}) %all-gather.5.cloned.1.call-update) | async-done | bytes 4194320 | tf_op jit(solution)/shard_map/all_gather | solution.py:30
  182.3 4.9 %fusion.16 = (f32[96]{0:T(128)S(1)}, f32[96]{0:T(128)S(1)}, f32[96]{0:T(128)S(1)}, bf16[96,128]{1,0:T(8,128)(2,1)S(1)}) fusion(s32[96,128]{1,0:T(8,128)S(1)} %copy-done.10, f32[96]{0:T(128)S(1)} %get-tuple-element.16, f32[96]{0:T(128)S(1)} %copy-done.13, bf16[16384,128]{0,1:T(8,128)(2,1)} %all-gather.5.cloned.1.call-done, bf16[96,16384]{1,0:T(8,128)(2,1)} %param.12), kind=kOutput, calls=%fused_computation.43 | convolution fusion | flops 403021536 | bytes 7415680 | tf_op jit(solution)/shard_map/dot_general | solution.py:31
  187.2 0.5 broadcast_multiply_fusion.3
  187.7 0.5 broadcast_multiply_fusion.1
  188.2 3.1 %fusion.1 = bf16[96,16384]{1,0:T(8,128)(2,1)} fusion(bf16[96,128]{1,0:T(8,128)(2,1)S(1)} %get-tuple-element.14, bf16[16384,128]{1,0:T(8,128)(2,1)S(1)} %copy-done.3), kind=kOutput, calls=%fused_computation.3 | convolution fusion | flops 405798912 | bytes 7364608 | tf_op jit(solution)/shard_map/dot_general | solution.py:34
  191.4 1.2 copy-done.4
  192.5 3.2 %fusion.2 = bf16[96,16384]{1,0:T(8,128)(2,1)} fusion(bf16[96,128]{1,0:T(8,128)(2,1)S(1)} %copy-done.8, bf16[16384,128]{0,1:T(8,128)(2,1)S(1)} %copy-done.2, f32[96,8192]{1,0:T(8,128)S(1)} %copy-done.5, f32[96,8192]{1,0:T(8,128)S(1)} %copy-done.4, f32[96]{0:T(128)S(1)} %get-tuple-element.21), kind=kOutput, calls=%fused_computation.4 | convolution fusion | flops 410517504 | bytes 13656448 | tf_op jit(solution)/shard_map/dot_general | solution.py:32
  (26 shorter events, 0.1 us)
Async XLA Ops:
  7.2 94.0 %copy-start = (bf16[96,16384]{1,0:T(8,128)(2,1)S(1)}, bf16[96,16384]{1,0:T(8,128)(2,1)}, u32[]{:S(2)}) copy-start(bf16[96,16384]{1,0:T(8,128)(2,1)} %param.9) | copy-start | bytes 9437188
  7.2 94.0 %all-gather.3.cloned.1.call-start = ((), (), s32[]{:S(2)}) async-start(), calls=%async_computation.1 | async-start | bytes 4456448 | tf_op jit(solution)/shard_map/all_gather | solution.py:20
  12.1 7.6 %copy-start.6 = (bf16[1024,128]{1,0:T(8,128)(2,1)S(1)}, bf16[1024,128]{1,0:T(8,128)(2,1)}, u32[]{:S(2)}) copy-start(bf16[1024,128]{1,0:T(8,128)(2,1)} %param.7) | copy-start | bytes 786436
  12.1 89.0 %copy-start.9 = (s32[96,128]{1,0:T(8,128)S(1)}, s32[96,128]{1,0:T(8,128)}, u32[]{:S(2)}) copy-start(s32[96,128]{1,0:T(8,128)} %param.8) | copy-start | bytes 147460
  12.1 89.0 %copy-start.12 = (f32[96]{0:T(128)S(1)}, f32[96]{0:T(128)}, u32[]{:S(2)}) copy-start(f32[96]{0:T(128)} %param.10) | copy-start | bytes 1156
  12.1 118.9 %all-to-all-start = ((bf16[96,16,1024]{2,0,1:T(8,128)(2,1)}), bf16[96,16,1024]{2,0,1:T(8,128)(2,1)}, u32[]{:S(2)}, u32[]{:S(2)}) async-start(bf16[96,16,1024]{2,0,1:T(8,128)(2,1)} %bitcast.26), calls=%async_computation | async-start | bytes 6291456 | tf_op jit(solution)/shard_map/all_to_all | solution.py:27
  19.7 162.6 %all-gather.5.cloned.1.call-start = ((), (), s32[]{:S(2)}) async-start(), calls=%async_computation.2 | async-start | bytes 4456448 | tf_op jit(solution)/shard_map/all_gather | solution.py:30
  20.6 110.4 %copy-start.11 = (f32[1024]{0:T(1024)S(1)}, f32[1024]{0:T(1024)}, u32[]{:S(2)}) copy-start(f32[1024]{0:T(1024)} %param.13) | copy-start | bytes 12292
  104.3 0.6 copy-start.7
  134.2 2.8 %copy-start.1 = (bf16[96,16384]{1,0:T(8,128)(2,1)S(1)}, bf16[96,16384]{1,0:T(8,128)(2,1)}, u32[]{:S(2)}) copy-start(bf16[96,16384]{1,0:T(8,128)(2,1)} %param.12) | copy-start | bytes 9437188
  137.1 45.2 %copy-start.10 = (s32[96,128]{1,0:T(8,128)S(1)}, s32[96,128]{1,0:T(8,128)}, u32[]{:S(2)}) copy-start(s32[96,128]{1,0:T(8,128)} %param.8) | copy-start | bytes 147460
  137.1 45.2 %copy-start.13 = (f32[96]{0:T(128)S(1)}, f32[96]{0:T(128)}, u32[]{:S(2)}) copy-start(f32[96]{0:T(128)} %param.11) | copy-start | bytes 1156
  182.3 6.0 %copy-start.3 = (bf16[16384,128]{1,0:T(8,128)(2,1)S(1)}, bf16[16384,128]{1,0:T(8,128)(2,1)}, u32[]{:S(2)}) copy-start(bf16[16384,128]{1,0:T(8,128)(2,1)} %all-gather.3.cloned.1.call-done) | copy-start | bytes 12582916
  182.3 9.1 %copy-start.5 = (f32[96,8192]{1,0:T(8,128)S(1)}, f32[96,8192]{1,0:T(8,128)}, u32[]{:S(2)}) copy-start(f32[96,8192]{1,0:T(8,128)} %get-tuple-element.12) | copy-start | bytes 9437188
  188.2 3.1 %copy-start.2 = (bf16[16384,128]{0,1:T(8,128)(2,1)S(1)}, bf16[16384,128]{0,1:T(8,128)(2,1)}, u32[]{:S(2)}) copy-start(bf16[16384,128]{0,1:T(8,128)(2,1)} %all-gather.5.cloned.1.call-done) | copy-start | bytes 12582916
  188.2 4.3 %copy-start.4 = (f32[96,8192]{1,0:T(8,128)S(1)}, f32[96,8192]{1,0:T(8,128)}, u32[]{:S(2)}) copy-start(f32[96,8192]{1,0:T(8,128)} %get-tuple-element.11) | copy-start | bytes 9437188
  188.2 4.3 %copy-start.8 = (bf16[96,128]{1,0:T(8,128)(2,1)S(1)}, bf16[96,128]{1,0:T(8,128)(2,1)}, u32[]{:S(2)}) copy-start(bf16[96,128]{1,0:T(8,128)(2,1)} %copy-done.7) | copy-start | bytes 73732
Sparse Core Ops, SparseCore 0:
  10.2 90.9 all-gather.2
  134.3 47.8 all-gather.4
where the time goes:
time: 203 us
  waiting for transfers between devices  122 us (60%)
  blocking collectives  26 us (13%)
  matrix products  17.7 us (9%)
  between operations  14.1 us (7%)
  other arithmetic  7.86 us (4%)
  starting transfers between devices  7.61 us (4%)
  local copies, waits for them, and re-layouts  6.93 us (3%)
    all_gather x1, waiting for transfers between devices, per_device(): gathered = lax.all_gather(acts, 'lat', axis=0, tiled=True)  80.6 us
    all_gather x1, waiting for transfers between devices, per_device(): all_errors = lax.all_gather(error, 'lat', axis=0, tiled=True)  41.1 us
    all_gather x1, blocking collectives, per_device(): all_feats = lax.all_gather(feats, 'lat', axis=0, tiled=True)  26 us
    all_to_all x1, starting transfers between devices, per_device(): lax.all_to_all(dec_weight, 'lat', split_axis=1, concat_axis=0, tiled=True)  7.53 us
    dot_general x1, matrix products, per_device(): grec = jnp.dot(dec_weight, all_errors, preferred_element_type=jnp.float32)  4.91 us
    all_to_all x1, local copies, waits for them, and re-layouts, per_device(): lax.all_to_all(dec_weight, 'lat', split_axis=1, concat_axis=0, tiled=True)  4.19 us
  transfers between devices with their start and end apart: 3, of which 2 were waited for; matrix products, arithmetic and copies ran while one was open for 7% of the time, Pallas kernels for 0%

commit v1 on v0

v1 whole, which is shorter than its diff:
```python
import functools
import math

import jax
import jax.numpy as jnp
from jax import lax
from jax.experimental import pallas as pl
from jax.experimental.pallas import tpu as pltpu
from jax.sharding import PartitionSpec as P

sparsity_coef = 0.1
spread = 0.1
norm_eps = 1e-06

MESH = pl.DeviceIdType.MESH
f32 = jnp.float32
bf16 = jnp.bfloat16


def lat_shape(lat):
    chips = lat // 2
    nx = 1
    while (2 * nx) ** 3 <= chips:
        nx *= 2
    return chips // nx, nx


def dot(a, b, dims):
    return lax.dot_general(a, b, (dims, ((), ())), preferred_element_type=f32)


NN = ((1,), (0,))
NT = ((1,), (1,))
TN = ((0,), (0,))


def kernel(
    nz, nx, scale,
    acts_ref, mask_ref, encb_ref, thr_ref, decb_ref, enc_hbm, dec_hbm,
    ge_out, geb_out, gth_out, gd_out, gdb_out,
    enc_v, dec_v, cat, abuf, ebuf, feats2, pre_v, grec_v, gpre_v, coef_v,
    bsend, brecv, csend, crecv, gd_v, ge_v, actst,
    load_sems, dsend, drecv, fsem,
    a_up, a_x, a_sib, a_recv, e_up, e_x, e_sib, e_recv,
    b_s, b_r, c_s, c_r, gd_sem, ge_sem,
):
    n = 2 * nz * nx
    rows = mask_ref.shape[0]
    fb = acts_ref.shape[0]
    me = lax.axis_index("lat")
    c = lax.rem(me, 2)
    x = lax.rem(me // 2, nx)
    z = me // (2 * nx)
    sib = me + 1 - 2 * c

    def at(zz, xx, cc):
        return (zz * nx + xx) * 2 + cc

    def shifted_x(d):
        return lax.rem(x + d, nx)

    def cols(i, width=fb):
        return pl.ds(pl.multiple_of(i * fb, 128), width)

    short = jnp.minimum(z, nz - 1 - z)
    upper = (2 * z < nz - 1).astype(jnp.int32)

    def kth(k):
        if k == 0:
            return z
        paired = z - (k + 1) // 2 if k % 2 else z + k // 2
        alone = z + (2 * upper - 1) * (k - short)
        both = (k <= 2 * short).astype(jnp.int32)
        return both * paired + (1 - both) * alone

    barrier = pltpu.get_barrier_semaphore()

    def greet(device):
        pl.semaphore_signal(barrier, inc=1, device_id={"lat": device}, device_id_type=MESH)

    has_down = z >= 1
    has_up = z <= nz - 2

    @pl.when(has_down)
    def _():
        greet(at(z - 1, x, c))

    @pl.when(has_up)
    def _():
        greet(at(z + 1, x, c))

    for d in range(1, nx):
        greet(at(z, shifted_x(d), c))
    greet(sib)

    loads = [
        pltpu.make_async_copy(enc_hbm, enc_v, load_sems.at[0]),
        pltpu.make_async_copy(dec_hbm, dec_v, load_sems.at[1]),
    ]
    for load in loads:
        load.start()

    pl.semaphore_wait(barrier, nx + has_down.astype(jnp.int32) + has_up.astype(jnp.int32))

    def remote(src, dst, send, recv, device):
        return pltpu.make_async_remote_copy(
            src_ref=src, dst_ref=dst, send_sem=send, recv_sem=recv,
            device_id={"lat": device}, device_id_type=MESH,
        )

    def block_copy(buf, i, send, recv, device):
        return remote(buf.at[i], buf.at[i], send, recv.at[i], device)

    def gather(buf, up_s, x_s, sib_s, recv, consume, first=None):
        def z_sends(k, zz):
            i = at(zz, x, c)
            go_up = jnp.logical_and(zz <= z, has_up)
            go_down = jnp.logical_and(zz >= z, has_down)
            return (
                (go_up, block_copy(buf, i, up_s.at[2 * k], recv, at(z + 1, x, c))),
                (go_down, block_copy(buf, i, up_s.at[2 * k + 1], recv, at(z - 1, x, c))),
            )

        def x_send(k, zz, d):
            return block_copy(buf, at(zz, x, c), x_s.at[k * nx + d], recv, at(z, shifted_x(d), c))

        def sib_send(k, zz, d):
            return block_copy(buf, at(zz, shifted_x(d), c), sib_s.at[k * nx + d], recv, sib)

        def arrived(i):
            block_copy(buf, i, sib_s.at[0], recv, sib).wait_recv()

        def step_z(k):
            zz = kth(k)
            if k:
                arrived(at(zz, x, c))
            for go, copy in z_sends(k, zz):
                @pl.when(go)
                def _(copy=copy):
                    copy.start()
            for d in range(1, nx):
                x_send(k, zz, d).start()
            sib_send(k, zz, 0).start()

        def step_x(k):
            zz = kth(k)
            for d in range(1, nx):
                arrived(at(zz, shifted_x(d), c))
                sib_send(k, zz, d).start()

        def step_sib(k):
            zz = kth(k)
            for d in range(nx):
                arrived(at(zz, shifted_x(d), 1 - c))
            consume(k, zz)

        for k in range(nz + 2):
            if k < nz:
                step_z(k)
            if k == 0 and first is not None:
                first()
            if 0 <= k - 1 < nz:
                step_x(k - 1)
            if 0 <= k - 2 < nz:
                step_sib(k - 2)

        for k in range(nz):
            zz = kth(k)
            for go, copy in z_sends(k, zz):
                @pl.when(go)
                def _(copy=copy):
                    copy.wait_send()
            for d in range(1, nx):
                x_send(k, zz, d).wait_send()
            for d in range(nx):
                sib_send(k, zz, d).wait_send()

    abuf[me] = acts_ref[...]

    def dec_send(q):
        return remote(
            dec_hbm.at[:, cols(2 * q + 1 - c)], cat.at[q, pl.ds(rows, rows), :],
            dsend.at[q], drecv.at[q], sib,
        )

    def dec_own(q):
        return pltpu.make_async_copy(
            dec_hbm.at[:, cols(2 * q + c)], cat.at[q, pl.ds(0, rows), :], load_sems.at[2 + q]
        )

    def eye():
        i = lax.broadcasted_iota(jnp.int32, (rows, rows), 0)
        j = lax.broadcasted_iota(jnp.int32, (rows, rows), 1)
        return i == j

    def column(row):
        return jnp.sum(jnp.where(eye(), jnp.broadcast_to(row, (rows, rows)), 0.0), axis=1, keepdims=True)

    def row_of(col):
        return jnp.sum(jnp.where(eye(), jnp.broadcast_to(col, (rows, rows)), 0.0), axis=0, keepdims=True)

    slab = 2 * nx

    def start_rest():
        for q in range(nz * nx):
            dec_own(q).start()
            dec_send(q).start()
        actst[...] = acts_ref[...].astype(f32).T
        pre_v[...] = jnp.zeros_like(pre_v)
        for load in loads:
            load.wait()

    def consume_acts(k, zz):
        def body(j, acc):
            i = zz * slab + j
            return acc + dot(enc_v[:, cols(i)], abuf[i], NN)
        pre_v[...] = lax.fori_loop(0, slab, body, pre_v[...], unroll=True)
        if k == 0:
            half = n // 2
            norms = []
            for m in range(2):
                def square(j, acc):
                    w = dec_v[:, cols(m * half + j)].astype(f32)
                    w = w * w
                    for t in range(fb // 128):
                        acc = acc + w[:, t * 128:(t + 1) * 128]
                    return acc
                acc = lax.fori_loop(0, half, square, jnp.zeros((rows, 128), f32))
                norms.append(jnp.sqrt(jnp.sum(acc, axis=1, keepdims=True) + norm_eps))
            active = lax.rem(mask_ref[...], 2).astype(f32)
            count = jnp.sum(active, axis=1, keepdims=True)
            lane = lax.broadcasted_iota(jnp.int32, (rows, 128), 1)
            coef_v[...] = jnp.where(
                lane == 0, sparsity_coef * count / norms[0],
                jnp.where(lane == 1, sparsity_coef * count / norms[1], norms[0] + norms[1]),
            )

    gather(abuf, a_up, a_x, a_sib, a_recv, consume_acts, start_rest)

    active = lax.rem(mask_ref[...], 2).astype(f32)
    pre = pre_v[...] + column(encb_ref[...])
    feats = (active * pre).astype(bf16)
    feats2[pl.ds(0, rows), :] = feats
    fcopy = remote(
        feats2.at[pl.ds(0, rows), :], feats2.at[pl.ds(rows, rows), :], fsem.at[0], fsem.at[1], sib
    )
    fcopy.start()
    for q in range(nz * nx):
        dec_own(q).wait()
        dec_send(q).wait()
    fcopy.wait()

    both = feats2[...]

    def partial(q):
        return dot(both, cat[q], TN)

    def b_copy(k, zz, d):
        return remote(
            bsend.at[k * nx + d], brecv.at[zz * nx + d], b_s.at[k * nx + d], b_r.at[zz * nx + d],
            at(z, shifted_x(d), c),
        )

    order = list(range(nz - 1, -1, -1))
    for k in order:
        zz = kth(k)
        for d in range(1, nx):
            bsend[k * nx + d] = partial(zz * nx + shifted_x(d)).astype(bf16)
            b_copy(k, zz, d).start()

    def c_copies(k, zz):
        down_slot = zz + (nz - zz) * (zz == z - 1).astype(jnp.int32)
        return (
            (zz > z, remote(csend.at[k], crecv.at[zz], c_s.at[k], c_r.at[zz], at(z + 1, x, c))),
            (zz < z, remote(csend.at[k], crecv.at[down_slot], c_s.at[k], c_r.at[down_slot], at(z - 1, x, c))),
        )

    def c_wait(slot):
        remote(csend.at[0], crecv.at[slot], c_s.at[0], c_r.at[slot], sib).wait_recv()

    total = actst
    for k in order:
        zz = kth(k)
        part = partial(zz * nx + x)
        for d in range(1, nx):
            b_copy(k, zz, d).wait_recv()
            part = part + brecv[zz * nx + d].astype(f32)
        if k:
            csend[k] = part.astype(bf16)
            farther = jnp.logical_or(
                jnp.logical_and(zz > z, has_down), jnp.logical_and(zz < z, has_up)
            )

            @pl.when(farther)
            def _(part=part, zz=zz, k=k):
                c_wait(zz)
                csend[k] = (part + crecv[zz].astype(f32)).astype(bf16)

            for go, copy in c_copies(k, zz):
                @pl.when(go)
                def _(copy=copy):
                    copy.start()
        else:
            total[...] = part + decb_ref[...] - total[...]

            @pl.when(has_down)
            def _():
                c_wait(z)
                total[...] += crecv[z].astype(f32)

            @pl.when(has_up)
            def _():
                c_wait(nz)
                total[...] += crecv[nz].astype(f32)

    error = total[...].astype(bf16)
    ebuf[me] = error

    def gd_copy(zz):
        w = cols(zz * slab, slab * fb)
        return pltpu.make_async_copy(gd_v.at[:, w], gd_out.at[:, w], gd_sem.at[zz])

    def finish_sums():
        gdb_out[...] = scale * jnp.sum(ebuf[me].astype(f32), axis=0, keepdims=True)
        grec_v[...] = jnp.zeros_like(grec_v)
        for k in range(nz):
            zz = kth(k)
            for d in range(1, nx):
                b_copy(k, zz, d).wait_send()
            if k:
                for go, copy in c_copies(k, zz):
                    @pl.when(go)
                    def _(copy=copy):
                        copy.wait_send()

    def consume_errors(k, zz):
        own = feats2[pl.ds(0, rows), :]

        def body(j, acc):
            i = zz * slab + j
            e = ebuf[i]
            w = dec_v[:, cols(i)]
            acc = acc + dot(w, e, NT)
            adjusted = (i >= n // 2).astype(f32)
            coef = coef_v[:, 0:1] + adjusted * (coef_v[:, 1:2] - coef_v[:, 0:1])
            gd_v[:, cols(i)] = (scale * (dot(own, e, NN) + coef * w.astype(f32))).astype(bf16)
            return acc

        grec_v[...] = lax.fori_loop(0, slab, body, grec_v[...])
        gd_copy(zz).start()

    gather(ebuf, e_up, e_x, e_sib, e_recv, consume_errors, finish_sums)

    grec = grec_v[...]
    active = lax.rem(mask_ref[...], 2).astype(f32)
    gpre = (active * grec).astype(bf16)
    gpre_v[...] = gpre

    def ge_copy(zz):
        w = cols(zz * slab, slab * fb)
        return pltpu.make_async_copy(ge_v.at[:, w], ge_out.at[:, w], ge_sem.at[zz])

    for zz in range(nz):
        def body(j, _):
            i = zz * slab + j
            ge_v[:, cols(i)] = (scale * dot(gpre_v[...], abuf[i], NT)).astype(bf16)
            return 0
        lax.fori_loop(0, slab, body, 0)
        ge_copy(zz).start()

    window = (mask_ref[...] // 2).astype(f32)
    theta = window * (column(thr_ref[...]) * grec + sparsity_coef * coef_v[:, 2:3])
    gth_out[...] = row_of(-(scale / spread) * jnp.sum(theta, axis=1, keepdims=True))
    geb_out[...] = row_of(scale * jnp.sum(gpre.astype(f32), axis=1, keepdims=True))
    for zz in range(nz):
        ge_copy(zz).wait()
        gd_copy(zz).wait()


def per_device(lat, acts, mask, enc_weight, enc_bias, threshold, dec_weight, dec_bias):
    nz, nx = lat_shape(lat)
    n = lat
    rows, tokens = mask.shape
    fb = acts.shape[0]
    width = dec_weight.shape[1]
    scale = 1.0 / math.sqrt(tokens)
    vmem = pl.BlockSpec(memory_space=pltpu.VMEM)
    hbm = pl.BlockSpec(memory_space=pl.ANY)
    dma = pltpu.SemaphoreType.DMA
    outs = pl.pallas_call(
        functools.partial(kernel, nz, nx, scale),
        out_shape=(
            jax.ShapeDtypeStruct((rows, width), bf16),
            jax.ShapeDtypeStruct((1, rows), f32),
            jax.ShapeDtypeStruct((1, rows), f32),
            jax.ShapeDtypeStruct((rows, width), bf16),
            jax.ShapeDtypeStruct((1, fb), f32),
        ),
        in_specs=[vmem] * 5 + [hbm] * 2,
        out_specs=(hbm, vmem, vmem, hbm, vmem),
        scratch_shapes=[
            pltpu.VMEM((rows, width), bf16),
            pltpu.VMEM((rows, width), bf16),
            pltpu.VMEM((nz * nx, 2 * rows, fb), bf16),
            pltpu.VMEM((n, fb, tokens), bf16),
            pltpu.VMEM((n, tokens, fb), bf16),
            pltpu.VMEM((2 * rows, tokens), bf16),
            pltpu.VMEM((rows, tokens), f32),
            pltpu.VMEM((rows, tokens), f32),
            pltpu.VMEM((rows, tokens), bf16),
            pltpu.VMEM((rows, 128), f32),
            pltpu.VMEM((nz * nx, tokens, fb), bf16),
            pltpu.VMEM((nz * nx, tokens, fb), bf16),
            pltpu.VMEM((nz, tokens, fb), bf16),
            pltpu.VMEM((nz + 1, tokens, fb), bf16),
            pltpu.VMEM((rows, width), bf16),
            pltpu.VMEM((rows, width), bf16),
            pltpu.VMEM((tokens, fb), f32),
            dma((2 + nz * nx,)), dma((nz * nx,)), dma((nz * nx,)), dma((2,)),
            dma((2 * nz,)), dma((nz * nx,)), dma((nz * nx,)), dma((n,)),
            dma((2 * nz,)), dma((nz * nx,)), dma((nz * nx,)), dma((n,)),
            dma((nz * nx,)), dma((nz * nx,)), dma((nz,)), dma((nz + 1,)),
            dma((nz,)), dma((nz,)),
        ],
        compiler_params=pltpu.CompilerParams(
            collective_id=0, has_side_effects=True, vmem_limit_bytes=56 * 1024 * 1024
        ),
        name="crosscoder",
    )(
        acts, mask, enc_bias.reshape(1, rows), threshold.reshape(1, rows),
        dec_bias.reshape(1, fb), enc_weight, dec_weight,
    )
    ge, geb, gth, gd, gdb = outs
    return ge, geb.reshape(rows), gth.reshape(rows), gd, gdb.reshape(fb)


def solution(mesh):
    wide, flat = P(("groups", "lat"), None), P(("groups", "lat"))
    return jax.shard_map(
        functools.partial(per_device, mesh.shape["lat"]), mesh=mesh,
        in_specs=(wide, wide, wide, flat, flat, wide, flat),
        out_specs=(wide, flat, flat, wide, flat), check_vma=False,
    )
```

time: 203 us -> 105 us (0.52)
  waiting for transfers between devices: 122 us -> 0 us
  Pallas kernels: 0 us -> 96.5 us
  blocking collectives: 26 us -> 0 us
  matrix products: 17.7 us -> 0 us
  between operations: 14.1 us -> 0.67 us
  other arithmetic: 7.86 us -> 0 us
  starting transfers between devices: 7.61 us -> 0 us
    all_gather x2 -> x0, waiting for transfers between devices: 122 us -> none  [the longest x1 80.6 us: per_device(): gathered = lax.all_gather(acts, 'lat', axis=0, tiled=True)]
    pallas_call x0 -> x1, Pallas kernels: none -> 96.5 us  [per_device(): pl.pallas_call(functools.partial(kernel, nz, nx, scale), out_shape=(jax.S...]
    all_gather x1 -> x0, blocking collectives: 26 us -> none  [per_device(): all_feats = lax.all_gather(feats, 'lat', axis=0, tiled=True)]
    dot_general x5 -> x0, matrix products: 17.7 us -> none  [the longest x1 4.91 us: per_device(): grec = jnp.dot(dec_weight, all_errors, preferred_element_type=jnp.float32)]
    all_to_all x1 -> x0, starting transfers between devices: 7.53 us -> none  [per_device(): lax.all_to_all(dec_weight, 'lat', split_axis=1, concat_axis=0, tiled=True)]
    unnamed x29 -> x13, local copies, waits for them, and re-layouts: 2.73 us -> 7.2 us
    all_to_all x1 -> x0, local copies, waits for them, and re-layouts: 4.19 us -> none  [per_device(): lax.all_to_all(dec_weight, 'lat', split_axis=1, concat_axis=0, tiled=True)]
    div x1 -> x0, other arithmetic: 3.49 us -> none  [per_device(): base_part / norm_base[:, None]]
  transfers between devices with their start and end apart: 3 -> 0, of which waited for: 2 -> 0; matrix products, arithmetic and copies ran while one was open for 7% -> 0% of each run, Pallas kernels for 0% -> 0%
where the time goes in v1:
time: 105 us; the launch traced here: 104 us
  Pallas kernels  96.5 us (92%)
  local copies, waits for them, and re-layouts  7.2 us (7%)
    pallas_call x1, Pallas kernels, per_device(): pl.pallas_call(functools.partial(kernel, nz, nx, scale), out_shape=(jax.S...  96.5 us
    unnamed x13, local copies, waits for them, and re-layouts  7.2 us

profile of v1, /device:TPU:0, one launch (start us, length us, event | category | flops | bytes accessed | tf_op | source)
XLA Modules:
  0.0 104.4 jit_solution(17585802757446338872)
XLA Ops:
  0.6 96.5 %crosscoder.1 = (bf16[96,16384]{1,0:T(8,128)(2,1)}, f32[1,96]{1,0:T(1,128)}, f32[1,96]{1,0:T(1,128)}, bf16[96,16384]{1,0:T(8,128)(2,1)}, f32[1,1024]{1,0:T(1,128)}) custom-call(bf16[1024,128]{1,0:T(8,128)(2,1)} %acts_ref.1, s32[96,128]{1,0:T(8,128)} %mask_ref.1, f32[1,96]{1,0:T(1,128)} %bitcast.8, f32[1,96]{1,0:T(1,128)} %bitcast.9, f32[1,1024]{1,0:T(1,128)} %bitcast.6, ...), custom_call_target="tpu_custom_call" | custom-call | tf_op jit(solution)/shard_map/crosscoder/pallas_call | solution.py:390
  97.2 0.0 copy-start.3
  97.2 0.0 copy-start.2
  97.2 0.0 copy-start
  97.2 3.9 %copy.17 = bf16[96,16384]{1,0:T(8,128)(2,1)} copy(bf16[96,16384]{1,0:T(8,128)(2,1)} %get-tuple-element.20) | data formatting | bytes 6291456
  101.1 0.0 copy-done.3
  101.1 0.5 copy.18
  101.6 0.0 copy-done.2
  101.6 0.5 copy.19
  102.1 0.0 copy-done
  102.1 0.0 copy-start.1
  102.2 1.7 %copy.20 = bf16[96,16384]{1,0:T(8,128)(2,1)} copy(bf16[96,16384]{1,0:T(8,128)(2,1)S(1)} %copy-done) | data formatting | bytes 6291456
  103.8 0.0 copy-done.1
  103.8 0.6 copy.21
Async XLA Ops:
  97.2 3.9 %copy-start.3 = (f32[1,96]{1,0:T(1,128)S(1)}, f32[1,96]{1,0:T(1,128)}, u32[]{:S(2)}) copy-start(f32[1,96]{1,0:T(1,128)} %get-tuple-element.11) | copy-start | bytes 1156
  97.2 4.4 %copy-start.2 = (f32[1,96]{1,0:T(1,128)S(1)}, f32[1,96]{1,0:T(1,128)}, u32[]{:S(2)}) copy-start(f32[1,96]{1,0:T(1,128)} %get-tuple-element.12) | copy-start | bytes 1156
  97.2 4.9 %copy-start = (bf16[96,16384]{1,0:T(8,128)(2,1)S(1)}, bf16[96,16384]{1,0:T(8,128)(2,1)}, u32[]{:S(2)}) copy-start(bf16[96,16384]{1,0:T(8,128)(2,1)} %get-tuple-element.23) | copy-start | bytes 9437188
  102.1 1.7 %copy-start.1 = (f32[1,1024]{1,0:T(1,128)S(1)}, f32[1,1024]{1,0:T(1,128)}, u32[]{:S(2)}) copy-start(f32[1,1024]{1,0:T(1,128)} %get-tuple-element.14) | copy-start | bytes 12292

commit v2 on v1

v2 whole, which is shorter than its diff:
```python
import functools
import math

import jax
import jax.numpy as jnp
from jax import lax
from jax.experimental import pallas as pl
from jax.experimental.pallas import tpu as pltpu
from jax.sharding import PartitionSpec as P

sparsity_coef = 0.1
spread = 0.1
norm_eps = 1e-06

MESH = pl.DeviceIdType.MESH
f32 = jnp.float32
bf16 = jnp.bfloat16


def lat_shape(lat):
    chips = lat // 2
    nx = 1
    while (2 * nx) ** 3 <= chips:
        nx *= 2
    return chips // nx, nx


def dot(a, b, dims):
    return lax.dot_general(a, b, (dims, ((), ())), preferred_element_type=f32)


NN = ((1,), (0,))
NT = ((1,), (1,))
TN = ((0,), (0,))


def kernel(
    nz, nx, parts, scale,
    acts_hbm, mask_hbm, encb_hbm, thr_hbm, decb_hbm, enc_hbm, dec_hbm,
    acts_out, gpre_out, geb_out, gth_out, gd_out, gdb_out,
    acts_ref, mask_ref, encb_ref, thr_ref, decb_ref, enc_v, dec_v, cat, abuf, ebuf, feats2, pre_v, grec_v, coef_v,
    bsend, brecv, csend, crecv, cpart, gd_v, actst,
    load_sems, dsend, drecv, fsem,
    a_up, a_x, a_sib, a_recv, e_up, e_x, e_sib, e_recv,
    b_s, b_r, c_s, c_r, gd_sem, out_sem,
):
    n = 2 * nz * nx
    rows = mask_hbm.shape[0]
    fb, tokens = acts_hbm.shape
    lag = 2 * parts
    me = lax.axis_index("lat")
    c = lax.rem(me, 2)
    x = lax.rem(me // 2, nx)
    z = me // (2 * nx)
    sib = me + 1 - 2 * c

    def at(zz, xx, cc):
        return (zz * nx + xx) * 2 + cc

    def shifted_x(d):
        return lax.rem(x + d, nx)

    def cols(i, width=fb):
        return pl.ds(pl.multiple_of(i * fb, 128), width)

    short = jnp.minimum(z, nz - 1 - z)
    upper = (2 * z < nz - 1).astype(jnp.int32)
    blocks, events = nz * parts, (nz - 1) * parts

    def place(paired, p, w, k, g):
        paired = paired.astype(jnp.int32)
        zz = paired * (z + (p + 1) * (2 * (w % 2) - 1)) + (1 - paired) * (z + (2 * upper - 1) * (k - short))
        k = paired * (2 * p + 1 + w % 2) + (1 - paired) * k
        g = paired * (w // 2) + (1 - paired) * g
        return k, zz, g

    def nearest_first(e):
        p, w = e // (2 * parts), e % (2 * parts)
        return place(p < short, p, w, 1 + e // parts, e % parts)

    def farthest_first(e):
        alone = (nz - 1 - 2 * short) * parts
        rest = jnp.maximum(e - alone, 0)
        p, w = short - 1 - rest // (2 * parts), rest % (2 * parts)
        return place(e >= alone, p, w, nz - 1 - e // parts, e % parts)

    def kth(k):
        if k == 0:
            return z
        paired = z - (k + 1) // 2 if k % 2 else z + k // 2
        alone = z + (2 * upper - 1) * (k - short)
        both = (k <= 2 * short).astype(jnp.int32)
        return both * paired + (1 - both) * alone

    def loop(count, body):
        def step(i, carry):
            body(i)
            return carry
        lax.fori_loop(0, count, step, 0)

    barrier = pltpu.get_barrier_semaphore()

    def greet(device):
        pl.semaphore_signal(barrier, inc=1, device_id={"lat": device}, device_id_type=MESH)

    has_down = z >= 1
    has_up = z <= nz - 2

    @pl.when(has_down)
    def _():
        greet(at(z - 1, x, c))

    @pl.when(has_up)
    def _():
        greet(at(z + 1, x, c))

    for d in range(1, nx):
        greet(at(z, shifted_x(d), c))
    greet(sib)

    acts_load, *loads = [
        pltpu.make_async_copy(src, dst, load_sems.at[nz * nx + i])
        for i, (src, dst) in enumerate((
            (acts_hbm, acts_ref), (mask_hbm, mask_ref), (encb_hbm, encb_ref), (thr_hbm, thr_ref),
            (decb_hbm, decb_ref), (enc_hbm, enc_v), (dec_hbm, dec_v),
        ))
    ]
    acts_load.start()
    for load in loads:
        load.start()
    acts_load.wait()
    actst[...] = acts_ref[...].astype(f32).T
    abuf[me] = actst[...].astype(bf16)

    pl.semaphore_wait(barrier, nx + has_down.astype(jnp.int32) + has_up.astype(jnp.int32))

    def remote(src, dst, send, recv, device):
        return pltpu.make_async_remote_copy(
            src_ref=src, dst_ref=dst, send_sem=send, recv_sem=recv,
            device_id={"lat": device}, device_id_type=MESH,
        )

    def gather(buf, up_s, x_s, sib_s, recv, consume, prepare, first=None):
        piece = buf.shape[1] // parts

        def copy_of(i, g, send, device):
            view = buf.at[i, pl.ds(pl.multiple_of(g * piece, piece), piece), :]
            return remote(view, view, send, recv.at[i, g], device)

        def event(e):
            k, zz, g = nearest_first(jnp.maximum(e - parts, 0))
            own = (e < parts).astype(jnp.int32)
            return zz + own * (z - zz), g + own * (e - g)

        def z_sends(e, zz, g):
            i = at(zz, x, c)
            go_up = jnp.logical_and(zz <= z, has_up)
            go_down = jnp.logical_and(zz >= z, has_down)
            return (
                (go_up, copy_of(i, g, up_s.at[0, e], at(z + 1, x, c))),
                (go_down, copy_of(i, g, up_s.at[1, e], at(z - 1, x, c))),
            )

        def x_send(e, zz, g, d):
            return copy_of(at(zz, x, c), g, x_s.at[d, e], at(z, shifted_x(d), c))

        def sib_send(e, zz, g, d):
            return copy_of(at(zz, shifted_x(d), c), g, sib_s.at[d, e], sib)

        def arrived(i, g):
            copy_of(i, g, sib_s.at[0, 0], sib).wait_recv()

        def send_on(e, zz, g):
            for go, copy in z_sends(e, zz, g):
                @pl.when(go)
                def _(copy=copy):
                    copy.start()
            for d in range(1, nx):
                x_send(e, zz, g, d).start()
            sib_send(e, zz, g, 0).start()

        def step_x(e):
            zz, g = event(e)
            for d in range(1, nx):
                arrived(at(zz, shifted_x(d), c), g)
                sib_send(e, zz, g, d).start()

        def step_sib(e):
            zz, g = event(e)
            for d in range(nx):
                arrived(at(zz, shifted_x(d), 1 - c), g)

            @pl.when(g == parts - 1)
            def _():
                consume(zz)

        for g in range(parts):
            prepare(g)
            send_on(g, z, g)
        if first is not None:
            first()

        def step(e):
            @pl.when(e < blocks)
            def _():
                zz, g = event(e)
                arrived(at(zz, x, c), g)
                send_on(e, zz, g)

            @pl.when(jnp.logical_and(e >= lag, e < blocks + lag))
            def _():
                step_x(e - lag)

            @pl.when(e >= lag + 2)
            def _():
                step_sib(e - lag - 2)

        loop(blocks + lag + 2 - parts, lambda i: step(i + parts))

        def settle(e):
            zz, g = event(e)
            for go, copy in z_sends(e, zz, g):
                @pl.when(go)
                def _(copy=copy):
                    copy.wait_send()
            for d in range(1, nx):
                x_send(e, zz, g, d).wait_send()
            for d in range(nx):
                sib_send(e, zz, g, d).wait_send()

        return lambda: loop(blocks, settle)


    def dec_send(q):
        return remote(
            dec_hbm.at[:, cols(2 * q + 1 - c)], cat.at[q, pl.ds(rows, rows), :],
            dsend.at[q], drecv.at[q], sib,
        )

    def dec_own(q):
        return pltpu.make_async_copy(
            dec_hbm.at[:, cols(2 * q + c)], cat.at[q, pl.ds(0, rows), :], load_sems.at[q]
        )

    def eye():
        i = lax.broadcasted_iota(jnp.int32, (rows, rows), 0)
        j = lax.broadcasted_iota(jnp.int32, (rows, rows), 1)
        return i == j

    def column(row):
        return jnp.sum(jnp.where(eye(), jnp.broadcast_to(row, (rows, rows)), 0.0), axis=1, keepdims=True)

    def row_of(col):
        return jnp.sum(jnp.where(eye(), jnp.broadcast_to(col, (rows, rows)), 0.0), axis=0, keepdims=True)

    slab = 2 * nx

    def start_rest():
        for q in range(nz * nx):
            dec_own(q).start()
            dec_send(q).start()
        pre_v[...] = jnp.zeros_like(pre_v)
        for load in loads:
            load.wait()

    def consume_acts(zz):
        acc = pre_v[...]
        for j in range(slab):
            i = zz * slab + j
            acc = acc + dot(enc_v[:, cols(i)], abuf[i], NT)
        pre_v[...] = acc

    def norms_and_counts():
        half = n // 2
        norms = []
        for m in range(2):
            def square(j, acc):
                w = dec_v[:, cols(m * half + j)].astype(f32)
                w = w * w
                for t in range(fb // 128):
                    acc = acc + w[:, t * 128:(t + 1) * 128]
                return acc
            acc = lax.fori_loop(0, half, square, jnp.zeros((rows, 128), f32))
            norms.append(jnp.sqrt(jnp.sum(acc, axis=1, keepdims=True) + norm_eps))
        active = lax.rem(mask_ref[...], 2).astype(f32)
        count = jnp.sum(active, axis=1, keepdims=True)
        lane = lax.broadcasted_iota(jnp.int32, (rows, 128), 1)
        coef_v[...] = jnp.where(
            lane == 0, sparsity_coef * count / norms[0],
            jnp.where(lane == 1, sparsity_coef * count / norms[1], norms[0] + norms[1]),
        )

    settle_acts = gather(abuf, a_up, a_x, a_sib, a_recv, consume_acts, lambda g: None, start_rest)

    active = lax.rem(mask_ref[...], 2).astype(f32)
    pre = pre_v[...] + column(encb_ref[...])
    feats = (active * pre).astype(bf16)
    feats2[pl.ds(0, rows), :] = feats
    fcopy = remote(
        feats2.at[pl.ds(0, rows), :], feats2.at[pl.ds(rows, rows), :], fsem.at[0], fsem.at[1], sib
    )
    fcopy.start()
    acts_copy = pltpu.make_async_copy(abuf, acts_out, out_sem.at[0])
    acts_copy.start()
    for q in range(nz * nx):
        dec_own(q).wait()
        dec_send(q).wait()
    fcopy.wait()

    both = feats2[...]

    def partial(q):
        return dot(both, cat[q], TN)

    piece = tokens // parts

    def lines(g):
        return pl.ds(pl.multiple_of(g * piece, piece), piece)

    def b_copy(k, zz, g, d):
        return remote(
            bsend.at[k * nx + d, lines(g), :], brecv.at[zz * nx + d, lines(g), :],
            b_s.at[k * nx + d, g], b_r.at[zz * nx + d, g], at(z, shifted_x(d), c),
        )

    def b_step(k, zz, g):
        for d in range(1, nx):
            @pl.when(g == 0)
            def _(d=d):
                bsend[k * nx + d] = partial(zz * nx + shifted_x(d)).astype(bf16)
            b_copy(k, zz, g, d).start()

    loop(events, lambda e: b_step(*farthest_first(e)))
    loop(parts, lambda g: b_step(0, z, g))
    for k in range(nz - 1, -1, -1):
        cpart[k] = partial(kth(k) * nx + x)
    settle_acts()
    norms_and_counts()

    def c_copies(k, zz, g):
        down_slot = zz + (nz - zz) * (zz == z - 1).astype(jnp.int32)
        return tuple(
            (go, remote(csend.at[k, lines(g), :], crecv.at[slot, lines(g), :], c_s.at[k, g], c_r.at[slot, g], device))
            for go, slot, device in ((zz > z, zz, at(z + 1, x, c)), (zz < z, down_slot, at(z - 1, x, c)))
        )

    def c_wait(slot, g):
        remote(csend.at[0, lines(g), :], crecv.at[slot, lines(g), :], c_s.at[0, g], c_r.at[slot, g], sib).wait_recv()

    def with_b(k, zz, g):
        part = cpart[k, lines(g), :]
        for d in range(1, nx):
            b_copy(k, zz, g, d).wait_recv()
            part = part + brecv[zz * nx + d, lines(g), :].astype(f32)
        return part

    def c_step(e):
        k, zz, g = farthest_first(e)
        part = with_b(k, zz, g)
        farther = jnp.logical_or(jnp.logical_and(zz > z, has_down), jnp.logical_and(zz < z, has_up))

        @pl.when(farther)
        def _():
            c_wait(zz, g)
            csend[k, lines(g), :] = (part + crecv[zz, lines(g), :].astype(f32)).astype(bf16)

        @pl.when(jnp.logical_not(farther))
        def _():
            csend[k, lines(g), :] = part.astype(bf16)

        for go, copy in c_copies(k, zz, g):
            @pl.when(go)
            def _(copy=copy):
                copy.start()

    loop(events, c_step)

    def prepare_error(g):
        actst[lines(g), :] = with_b(0, z, g) + decb_ref[...] - actst[lines(g), :]

        @pl.when(has_down)
        def _():
            c_wait(z, g)
            actst[lines(g), :] += crecv[z, lines(g), :].astype(f32)

        @pl.when(has_up)
        def _():
            c_wait(nz, g)
            actst[lines(g), :] += crecv[nz, lines(g), :].astype(f32)

        ebuf[me, lines(g), :] = actst[lines(g), :].astype(bf16)

    def gd_copy(zz):
        w = cols(zz * slab, slab * fb)
        return pltpu.make_async_copy(gd_v.at[:, w], gd_out.at[:, w], gd_sem.at[zz])

    def finish_sums():
        gdb_out[...] = scale * jnp.sum(ebuf[me].astype(f32), axis=0, keepdims=True)
        grec_v[...] = jnp.zeros_like(grec_v)

        def settle(k, zz, g):
            for d in range(1, nx):
                b_copy(k, zz, g, d).wait_send()

        def settle_c(e):
            k, zz, g = farthest_first(e)
            settle(k, zz, g)
            for go, copy in c_copies(k, zz, g):
                @pl.when(go)
                def _(copy=copy):
                    copy.wait_send()

        loop(events, settle_c)
        loop(parts, lambda g: settle(0, z, g))

    def consume_errors(zz):
        own = feats2[pl.ds(0, rows), :]

        def body(j, acc):
            i = zz * slab + j
            e = ebuf[i]
            w = dec_v[:, cols(i)]
            acc = acc + dot(w, e, NT)
            adjusted = (i >= n // 2).astype(f32)
            coef = coef_v[:, 0:1] + adjusted * (coef_v[:, 1:2] - coef_v[:, 0:1])
            gd_v[:, cols(i)] = (scale * (dot(own, e, NN) + coef * w.astype(f32))).astype(bf16)
            return acc

        grec_v[...] = lax.fori_loop(0, slab, body, grec_v[...])
        gd_copy(zz).start()

    settle_errors = gather(ebuf, e_up, e_x, e_sib, e_recv, consume_errors, prepare_error, finish_sums)

    grec = grec_v[...]
    active = lax.rem(mask_ref[...], 2).astype(f32)
    gpre = (active * grec).astype(bf16)
    gpre_out[...] = gpre
    window = (mask_ref[...] // 2).astype(f32)
    theta = window * (column(thr_ref[...]) * grec + sparsity_coef * coef_v[:, 2:3])
    gth_out[...] = row_of(-(scale / spread) * jnp.sum(theta, axis=1, keepdims=True))
    geb_out[...] = row_of(scale * jnp.sum(gpre.astype(f32), axis=1, keepdims=True))
    settle_errors()
    acts_copy.wait()
    for zz in range(nz):
        gd_copy(zz).wait()


def finish(scale, acts_ref, gpre_ref, gd_ref, geb_ref, gth_ref, gdb_ref, ge_o, gd_o, geb_o, gth_o, gdb_o):
    fb = acts_ref.shape[2]
    for j in range(acts_ref.shape[0]):
        ge_o[:, j * fb:(j + 1) * fb] = (scale * dot(gpre_ref[...], acts_ref[j], NN)).astype(bf16)
    gd_o[...] = gd_ref[...]
    geb_o[...] = geb_ref[...]
    gth_o[...] = gth_ref[...]
    gdb_o[...] = gdb_ref[...]


def per_device(lat, acts, mask, enc_weight, enc_bias, threshold, dec_weight, dec_bias):
    nz, nx = lat_shape(lat)
    n = lat
    rows, tokens = mask.shape
    fb = acts.shape[0]
    width = dec_weight.shape[1]
    scale = 1.0 / math.sqrt(tokens)
    vmem = pl.BlockSpec(memory_space=pltpu.VMEM)
    hbm = pl.BlockSpec(memory_space=pl.ANY)
    parts = 2
    dma = pltpu.SemaphoreType.DMA
    outs = pl.pallas_call(
        functools.partial(kernel, nz, nx, parts, scale),
        out_shape=(
            jax.ShapeDtypeStruct((n, tokens, fb), bf16),
            jax.ShapeDtypeStruct((rows, tokens), bf16),
            jax.ShapeDtypeStruct((1, rows), f32),
            jax.ShapeDtypeStruct((1, rows), f32),
            jax.ShapeDtypeStruct((rows, width), bf16),
            jax.ShapeDtypeStruct((1, fb), f32),
        ),
        in_specs=[hbm] * 7,
        out_specs=(hbm, vmem, vmem, vmem, hbm, vmem),
        scratch_shapes=[
            pltpu.VMEM((fb, tokens), bf16),
            pltpu.VMEM((rows, tokens), jnp.int32),
            pltpu.VMEM((1, rows), f32),
            pltpu.VMEM((1, rows), f32),
            pltpu.VMEM((1, fb), f32),
            pltpu.VMEM((rows, width), bf16),
            pltpu.VMEM((rows, width), bf16),
            pltpu.VMEM((nz * nx, 2 * rows, fb), bf16),
            pltpu.VMEM((n, tokens, fb), bf16),
            pltpu.VMEM((n, tokens, fb), bf16),
            pltpu.VMEM((2 * rows, tokens), bf16),
            pltpu.VMEM((rows, tokens), f32),
            pltpu.VMEM((rows, tokens), f32),
            pltpu.VMEM((rows, 128), f32),
            pltpu.VMEM((nz * nx, tokens, fb), bf16),
            pltpu.VMEM((nz * nx, tokens, fb), bf16),
            pltpu.VMEM((nz, tokens, fb), bf16),
            pltpu.VMEM((nz + 1, tokens, fb), bf16),
            pltpu.VMEM((nz, tokens, fb), f32),
            pltpu.VMEM((rows, width), bf16),
            pltpu.VMEM((tokens, fb), f32),
            dma((7 + nz * nx,)), dma((nz * nx,)), dma((nz * nx,)), dma((2,)),
            dma((2, nz * parts)), dma((nx, nz * parts)), dma((nx, nz * parts)), dma((n, parts)),
            dma((2, nz * parts)), dma((nx, nz * parts)), dma((nx, nz * parts)), dma((n, parts)),
            dma((nz * nx, parts)), dma((nz * nx, parts)), dma((nz, parts)), dma((nz + 1, parts)),
            dma((nz,)), dma((1,)),
        ],
        compiler_params=pltpu.CompilerParams(
            collective_id=0, has_side_effects=True, vmem_limit_bytes=56 * 1024 * 1024
        ),
        name="crosscoder",
    )(
        acts, mask, enc_bias.reshape(1, rows), threshold.reshape(1, rows),
        dec_bias.reshape(1, fb), enc_weight, dec_weight,
    )
    all_acts, gpre, geb, gth, gd, gdb = outs
    steps = 8
    block = width // steps
    held = lambda shape: pl.BlockSpec(shape, lambda i: (0, 0))
    across = pl.BlockSpec((rows, block), lambda i: (0, i))
    small = [held((1, rows)), held((1, rows)), held((1, fb))]
    ge, gd, geb, gth, gdb = pl.pallas_call(
        functools.partial(finish, scale),
        grid=(steps,),
        out_shape=(
            jax.ShapeDtypeStruct((rows, width), bf16),
            jax.ShapeDtypeStruct((rows, width), bf16),
            jax.ShapeDtypeStruct((1, rows), f32),
            jax.ShapeDtypeStruct((1, rows), f32),
            jax.ShapeDtypeStruct((1, fb), f32),
        ),
        in_specs=[pl.BlockSpec((n // steps, tokens, fb), lambda i: (i, 0, 0)), held((rows, tokens)), across] + small,
        out_specs=[across, across] + small,
        compiler_params=pltpu.CompilerParams(vmem_limit_bytes=60 * 1024 * 1024),
        name="last_products",
    )(all_acts, gpre, gd, geb, gth, gdb)
    return ge, geb.reshape(rows), gth.reshape(rows), gd, gdb.reshape(fb)


def solution(mesh):
    wide, flat = P(("groups", "lat"), None), P(("groups", "lat"))
    return jax.shard_map(
        functools.partial(per_device, mesh.shape["lat"]), mesh=mesh,
        in_specs=(wide, wide, wide, flat, flat, wide, flat),
        out_specs=(wide, flat, flat, wide, flat), check_vma=False,
    )
```

time: 105 us -> 92.4 us (0.88)
  local copies, waits for them, and re-layouts: 7.2 us -> 0 us
  Pallas kernels: 96.5 us -> 91.4 us
    unnamed x13 -> x0, local copies, waits for them, and re-layouts: 7.2 us -> none
    pallas_call x1 -> x2, Pallas kernels: 96.5 us -> 91.4 us  [the longest x1 82.9 us: per_device(): pl.pallas_call(functools.partial(kernel, nz, nx, parts, scale), out_shape...]
where the time goes in v2:
time: 92.4 us; the launch traced here: 92.1 us
  Pallas kernels  91.4 us (99%)
    pallas_call x1, Pallas kernels, per_device(): pl.pallas_call(functools.partial(kernel, nz, nx, parts, scale), out_shape...  82.9 us
    pallas_call x1, Pallas kernels, per_device(): pl.pallas_call(functools.partial(finish, scale), grid=(steps,), out_shape...  8.53 us

profile of v2, /device:TPU:0, one launch (start us, length us, event | category | flops | bytes accessed | tf_op | source)
XLA Modules:
  0.0 92.1 jit_solution(13379500646304213934)
XLA Ops:
  0.6 82.9 %crosscoder.1 = (bf16[16,128,1024]{2,1,0:T(8,128)(2,1)}, bf16[96,128]{1,0:T(8,128)(2,1)}, f32[1,96]{1,0:T(1,128)}, f32[1,96]{1,0:T(1,128)}, bf16[96,16384]{1,0:T(8,128)(2,1)}, /*index=5*/f32[1,1024]{1,0:T(1,128)}) custom-call(bf16[1024,128]{1,0:T(8,128)(2,1)} %acts_hbm.1, s32[96,128]{1,0:T(8,128)} %mask_hbm.1, f32[1,96]{1,0:T(1,128)} %bitcast.7, ...), custom_call_target="tpu_custom_call" | custom-call | tf_op jit(solution)/shard_map/crosscoder/pallas_call | solution.py:469
  83.6 8.5 %last_products.1 = (bf16[96,16384]{1,0:T(8,128)(2,1)}, bf16[96,16384]{1,0:T(8,128)(2,1)}, f32[1,96]{1,0:T(1,128)}, f32[1,96]{1,0:T(1,128)}, f32[1,1024]{1,0:T(1,128)}) custom-call(bf16[16,128,1024]{2,1,0:T(8,128)(2,1)} %get-tuple-element.16.acts_ref, bf16[96,128]{1,0:T(8,128)(2,1)} %get-tuple-element.17.gpre_ref, ...), custom_call_target="tpu_custom_call" | custom-call | tf_op jit(solution)/shard_map/last_products/pallas_call | solution.py:523

commit v3 on v2

--- a/solution.py
+++ b/solution.py
@@ -47,7 +47,6 @@
     n = 2 * nz * nx
     rows = mask_hbm.shape[0]
     fb, tokens = acts_hbm.shape
-    lag = 2 * parts
     me = lax.axis_index("lat")
     c = lax.rem(me, 2)
     x = lax.rem(me // 2, nx)
@@ -65,7 +64,7 @@
 
     short = jnp.minimum(z, nz - 1 - z)
     upper = (2 * z < nz - 1).astype(jnp.int32)
-    blocks, events = nz * parts, (nz - 1) * parts
+    events = (nz - 1) * parts
 
     def place(paired, p, w, k, g):
         paired = paired.astype(jnp.int32)
@@ -74,7 +73,7 @@
         g = paired * (w // 2) + (1 - paired) * g
         return k, zz, g
 
-    def nearest_first(e):
+    def nearest_first(e, parts=3):
         p, w = e // (2 * parts), e % (2 * parts)
         return place(p < short, p, w, 1 + e // parts, e % parts)
 
@@ -140,25 +139,35 @@
             device_id={"lat": device}, device_id_type=MESH,
         )
 
-    def gather(buf, up_s, x_s, sib_s, recv, consume, prepare, first=None):
-        piece = buf.shape[1] // parts
+    def gather(buf, up_s, x_s, sib_s, recv, consume, prepare, first):
+        height = buf.shape[1]
+        thin, half = height // 8, height // 2
+        spans = ((thin, half - thin), (half, height - half), (0, thin))
+        pieces, wide = len(spans), len(spans) - 1
+        blocks, lag = nz * pieces, 2 * pieces
 
         def copy_of(i, g, send, device):
-            view = buf.at[i, pl.ds(pl.multiple_of(g * piece, piece), piece), :]
+            view = buf.at[i, pl.ds(*spans[g]), :]
             return remote(view, view, send, recv.at[i, g], device)
 
         def event(e):
-            k, zz, g = nearest_first(jnp.maximum(e - parts, 0))
-            own = (e < parts).astype(jnp.int32)
+            k, zz, g = nearest_first(jnp.maximum(e - pieces, 0))
+            own = (e < pieces).astype(jnp.int32)
             return zz + own * (z - zz), g + own * (e - g)
 
-        def z_sends(e, zz, g):
-            i = at(zz, x, c)
+        def by_piece(g, act):
+            for s in range(pieces):
+                @pl.when(g == s)
+                def _(s=s):
+                    act(s)
+
+        def z_sends(e, zz, g, d):
+            i = at(zz, shifted_x(d), c)
             go_up = jnp.logical_and(zz <= z, has_up)
             go_down = jnp.logical_and(zz >= z, has_down)
             return (
-                (go_up, copy_of(i, g, up_s.at[0, e], at(z + 1, x, c))),
-                (go_down, copy_of(i, g, up_s.at[1, e], at(z - 1, x, c))),
+                (go_up, copy_of(i, g, up_s.at[0, d, e], at(z + 1, x, c))),
+                (go_down, copy_of(i, g, up_s.at[1, d, e], at(z - 1, x, c))),
             )
 
         def x_send(e, zz, g, d):
@@ -170,65 +179,101 @@
         def arrived(i, g):
             copy_of(i, g, sib_s.at[0, 0], sib).wait_recv()
 
-        def send_on(e, zz, g):
-            for go, copy in z_sends(e, zz, g):
+        def along(e, zz, g, d):
+            for go, copy in z_sends(e, zz, g, d):
                 @pl.when(go)
                 def _(copy=copy):
                     copy.start()
+
+        def across(e, zz, g):
             for d in range(1, nx):
                 x_send(e, zz, g, d).start()
-            sib_send(e, zz, g, 0).start()
+
+        def step_z(e):
+            zz, piece = event(e)
+
+            def act(g):
+                for d in range(nx if g == wide else 1):
+                    arrived(at(zz, shifted_x(d), c), g)
+                    along(e, zz, g, d)
+                    if g != wide:
+                        across(e, zz, g)
+                    sib_send(e, zz, g, d).start()
+
+            by_piece(piece, act)
 
         def step_x(e):
-            zz, g = event(e)
-            for d in range(1, nx):
-                arrived(at(zz, shifted_x(d), c), g)
-                sib_send(e, zz, g, d).start()
+            zz, piece = event(e)
+
+            def act(g):
+                for d in range(1, nx if g != wide else 1):
+                    arrived(at(zz, shifted_x(d), c), g)
+                    sib_send(e, zz, g, d).start()
+
+            by_piece(piece, act)
 
         def step_sib(e):
-            zz, g = event(e)
-            for d in range(nx):
-                arrived(at(zz, shifted_x(d), 1 - c), g)
-
-            @pl.when(g == parts - 1)
+            zz, piece = event(e)
+
+            def act(g):
+                for d in range(nx):
+                    arrived(at(zz, shifted_x(d), 1 - c), g)
+
+            by_piece(piece, act)
+
+            @pl.when(piece == pieces - 1)
             def _():
                 consume(zz)
 
-        for g in range(parts):
+        for g in (wide, 0, 1):
             prepare(g)
-            send_on(g, z, g)
-        if first is not None:
-            first()
+            across(g, z, g)
+            along(g, z, g, 0)
+            sib_send(g, z, g, 0).start()
+        for d in range(1, nx):
+            arrived(at(z, shifted_x(d), c), wide)
+            along(wide, z, wide, d)
+            sib_send(wide, z, wide, d).start()
+        first()
 
         def step(e):
             @pl.when(e < blocks)
             def _():
-                zz, g = event(e)
-                arrived(at(zz, x, c), g)
-                send_on(e, zz, g)
+                step_z(e)
 
             @pl.when(jnp.logical_and(e >= lag, e < blocks + lag))
             def _():
                 step_x(e - lag)
 
-            @pl.when(e >= lag + 2)
+            @pl.when(e >= lag + 1)
             def _():
-                step_sib(e - lag - 2)
-
-        loop(blocks + lag + 2 - parts, lambda i: step(i + parts))
+                step_sib(e - lag - 1)
+
+        loop(blocks + lag + 1 - pieces, lambda i: step(i + pieces))
 
         def settle(e):
-            zz, g = event(e)
-            for go, copy in z_sends(e, zz, g):
-                @pl.when(go)
-                def _(copy=copy):
-                    copy.wait_send()
+            zz, piece = event(e)
+
+            def act(g):
+                for d in range(nx if g == wide else 1):
+                    for go, copy in z_sends(e, zz, g, d):
+                        @pl.when(go)
+                        def _(copy=copy):
+                            copy.wait_send()
+                for d in range(nx):
+                    sib_send(e, zz, g, d).wait_send()
+                if g != wide:
+                    for d in range(1, nx):
+                        x_send(e, zz, g, d).wait_send()
+
+            by_piece(piece, act)
+
+        def settle_all():
             for d in range(1, nx):
-                x_send(e, zz, g, d).wait_send()
-            for d in range(nx):
-                sib_send(e, zz, g, d).wait_send()
-
-        return lambda: loop(blocks, settle)
+                x_send(wide, z, wide, d).wait_send()
+            loop(blocks, settle)
+
+        return settle_all
 
 
     def dec_send(q):
@@ -375,7 +420,10 @@
 
     loop(events, c_step)
 
-    def prepare_error(g):
+    def prepare_error(piece):
+        if piece == 0:
+            return
+        g = 2 - piece
         actst[lines(g), :] = with_b(0, z, g) + decb_ref[...] - actst[lines(g), :]
 
         @pl.when(has_down)
@@ -445,14 +493,51 @@
         gd_copy(zz).wait()
 
 
-def finish(scale, acts_ref, gpre_ref, gd_ref, geb_ref, gth_ref, gdb_ref, ge_o, gd_o, geb_o, gth_o, gdb_o):
-    fb = acts_ref.shape[2]
-    for j in range(acts_ref.shape[0]):
-        ge_o[:, j * fb:(j + 1) * fb] = (scale * dot(gpre_ref[...], acts_ref[j], NN)).astype(bf16)
-    gd_o[...] = gd_ref[...]
+def finish(
+    scale, acts_in, gpre_ref, gd_in, geb_ref, gth_ref, gdb_ref, ge_out, gd_out, geb_o, gth_o, gdb_o,
+    acts_v, gd_v, ge_v, gd_r, gd_w, acts_r, ge_w,
+):
+    steps, strips = acts_r.shape[0], gd_r.shape[0]
+    per, fb = acts_v.shape[0] // steps, acts_v.shape[2]
+    tall = gd_v.shape[0] // strips
+
+    def gd_read(i):
+        rows = pl.ds(i * tall, tall)
+        return pltpu.make_async_copy(gd_in.at[rows, :], gd_v.at[rows, :], gd_r.at[i])
+
+    def gd_write(i):
+        rows = pl.ds(i * tall, tall)
+        return pltpu.make_async_copy(gd_v.at[rows, :], gd_out.at[rows, :], gd_w.at[i])
+
+    def acts_read(i):
+        some = pl.ds(i * per, per)
+        return pltpu.make_async_copy(acts_in.at[some], acts_v.at[some], acts_r.at[i])
+
+    def ge_write(i):
+        w = pl.ds(i * per * fb, per * fb)
+        return pltpu.make_async_copy(ge_v.at[:, w], ge_out.at[:, w], ge_w.at[i])
+
+    for i in range(max(steps, strips)):
+        if i < strips:
+            gd_read(i).start()
+        if i < steps:
+            acts_read(i).start()
     geb_o[...] = geb_ref[...]
     gth_o[...] = gth_ref[...]
     gdb_o[...] = gdb_ref[...]
+    for i in range(max(steps, strips)):
+        if i < strips:
+            gd_read(i).wait()
+            gd_write(i).start()
+        if i < steps:
+            acts_read(i).wait()
+            for j in range(i * per, (i + 1) * per):
+                ge_v[:, j * fb:(j + 1) * fb] = (scale * dot(gpre_ref[...], acts_v[j], NN)).astype(bf16)
+            ge_write(i).start()
+    for i in range(strips):
+        gd_write(i).wait()
+    for i in range(steps):
+        ge_write(i).wait()
 
 
 def per_device(lat, acts, mask, enc_weight, enc_bias, threshold, dec_weight, dec_bias):
@@ -501,8 +586,8 @@
             pltpu.VMEM((rows, width), bf16),
             pltpu.VMEM((tokens, fb), f32),
             dma((7 + nz * nx,)), dma((nz * nx,)), dma((nz * nx,)), dma((2,)),
-            dma((2, nz * parts)), dma((nx, nz * parts)), dma((nx, nz * parts)), dma((n, parts)),
-            dma((2, nz * parts)), dma((nx, nz * parts)), dma((nx, nz * parts)), dma((n, parts)),
+            dma((2, nx, nz * 3)), dma((nx, nz * 3)), dma((nx, nz * 3)), dma((n, 3)),
+            dma((2, nx, nz * 3)), dma((nx, nz * 3)), dma((nx, nz * 3)), dma((n, 3)),
             dma((nz * nx, parts)), dma((nz * nx, parts)), dma((nz, parts)), dma((nz + 1, parts)),
             dma((nz,)), dma((1,)),
         ],
@@ -515,14 +600,9 @@
         dec_bias.reshape(1, fb), enc_weight, dec_weight,
     )
     all_acts, gpre, geb, gth, gd, gdb = outs
-    steps = 8
-    block = width // steps
-    held = lambda shape: pl.BlockSpec(shape, lambda i: (0, 0))
-    across = pl.BlockSpec((rows, block), lambda i: (0, i))
-    small = [held((1, rows)), held((1, rows)), held((1, fb))]
+    steps, strips = 8, rows // 16
     ge, gd, geb, gth, gdb = pl.pallas_call(
         functools.partial(finish, scale),
-        grid=(steps,),
         out_shape=(
             jax.ShapeDtypeStruct((rows, width), bf16),
             jax.ShapeDtypeStruct((rows, width), bf16),
@@ -530,8 +610,12 @@
             jax.ShapeDtypeStruct((1, rows), f32),
             jax.ShapeDtypeStruct((1, fb), f32),
         ),
-        in_specs=[pl.BlockSpec((n // steps, tokens, fb), lambda i: (i, 0, 0)), held((rows, tokens)), across] + small,
-        out_specs=[across, across] + small,
+        in_specs=[hbm, vmem, hbm] + [vmem] * 3,
+        out_specs=(hbm, hbm, vmem, vmem, vmem),
+        scratch_shapes=[
+            pltpu.VMEM((n, tokens, fb), bf16), pltpu.VMEM((rows, width), bf16), pltpu.VMEM((rows, width), bf16),
+            dma((strips,)), dma((strips,)), dma((steps,)), dma((steps,)),
+        ],
         compiler_params=pltpu.CompilerParams(vmem_limit_bytes=60 * 1024 * 1024),
         name="last_products",
     )(all_acts, gpre, gd, geb, gth, gdb)

time: 92.4 us -> 90 us (0.974)
  Pallas kernels: 91.4 us -> 89.1 us
    pallas_call x1, Pallas kernels: 82.9 us -> 81.7 us  [per_device(): pl.pallas_call(functools.partial(kernel, nz, nx, parts, scale), out_shape...]
    pallas_call x1, Pallas kernels: 8.53 us -> 7.37 us  [per_device(): pl.pallas_call(functools.partial(finish, scale), out_shape=(jax.ShapeDtyp...]
where the time goes in v3:
time: 90 us; the launch traced here: 89.7 us
  Pallas kernels  89.1 us (99%)
    pallas_call x1, Pallas kernels, per_device(): pl.pallas_call(functools.partial(kernel, nz, nx, parts, scale), out_shape...  81.7 us
    pallas_call x1, Pallas kernels, per_device(): pl.pallas_call(functools.partial(finish, scale), out_shape=(jax.ShapeDtyp...  7.37 us

profile of v3, /device:TPU:0, one launch (start us, length us, event | category | flops | bytes accessed | tf_op | source)
XLA Modules:
  0.0 89.7 jit_solution(9591136997583749967)
XLA Ops:
  0.6 81.7 %crosscoder.1 = (bf16[16,128,1024]{2,1,0:T(8,128)(2,1)}, bf16[96,128]{1,0:T(8,128)(2,1)}, f32[1,96]{1,0:T(1,128)}, f32[1,96]{1,0:T(1,128)}, bf16[96,16384]{1,0:T(8,128)(2,1)}, /*index=5*/f32[1,1024]{1,0:T(1,128)}) custom-call(bf16[1024,128]{1,0:T(8,128)(2,1)} %acts_hbm.1, s32[96,128]{1,0:T(8,128)} %mask_hbm.1, f32[1,96]{1,0:T(1,128)} %bitcast.7, ...), custom_call_target="tpu_custom_call" | custom-call | tf_op jit(solution)/shard_map/crosscoder/pallas_call | solution.py:554
  82.3 7.4 %last_products.1 = (bf16[96,16384]{1,0:T(8,128)(2,1)}, bf16[96,16384]{1,0:T(8,128)(2,1)}, f32[1,96]{1,0:T(1,128)}, f32[1,96]{1,0:T(1,128)}, f32[1,1024]{1,0:T(1,128)}) custom-call(bf16[16,128,1024]{2,1,0:T(8,128)(2,1)} %get-tuple-element.16.acts_in, bf16[96,128]{1,0:T(8,128)(2,1)} %get-tuple-element.17.gpre_ref, bf16[96,16384]{1,0:T(8,128)(2,1)} %get-tuple-element.18.gd_in, ...), custom_call_target="tpu_custom_call" | custom-call | tf_op jit(solution)/shard_map/last_products/pallas_call | solution.py:604

commit v4 on v3

--- a/solution.py
+++ b/solution.py
@@ -474,7 +474,7 @@
             gd_v[:, cols(i)] = (scale * (dot(own, e, NN) + coef * w.astype(f32))).astype(bf16)
             return acc
 
-        grec_v[...] = lax.fori_loop(0, slab, body, grec_v[...])
+        grec_v[...] = lax.fori_loop(0, slab, body, grec_v[...], unroll=True)
         gd_copy(zz).start()
 
     settle_errors = gather(ebuf, e_up, e_x, e_sib, e_recv, consume_errors, prepare_error, finish_sums)
@@ -518,10 +518,10 @@
         return pltpu.make_async_copy(ge_v.at[:, w], ge_out.at[:, w], ge_w.at[i])
 
     for i in range(max(steps, strips)):
+        if i < steps:
+            acts_read(i).start()
         if i < strips:
             gd_read(i).start()
-        if i < steps:
-            acts_read(i).start()
     geb_o[...] = geb_ref[...]
     gth_o[...] = gth_ref[...]
     gdb_o[...] = gdb_ref[...]

time: 90 us -> 89.6 us (level)
  Pallas kernels: 89.1 us -> 87.9 us
    pallas_call x1, Pallas kernels: 81.7 us -> 80.5 us  [per_device(): pl.pallas_call(functools.partial(kernel, nz, nx, parts, scale), out_shape...]
where the time goes in v4:
time: 89.6 us; the launch traced here: 88.5 us
  Pallas kernels  87.9 us (98%)
    pallas_call x1, Pallas kernels, per_device(): pl.pallas_call(functools.partial(kernel, nz, nx, parts, scale), out_shape...  80.5 us
    pallas_call x1, Pallas kernels, per_device(): pl.pallas_call(functools.partial(finish, scale), out_shape=(jax.ShapeDtyp...  7.37 us

profile of v4, /device:TPU:0, one launch (start us, length us, event | category | flops | bytes accessed | tf_op | source)
XLA Modules:
  0.0 88.5 jit_solution(2896142123818848067)
XLA Ops:
  0.6 80.5 %crosscoder.1 = (bf16[16,128,1024]{2,1,0:T(8,128)(2,1)}, bf16[96,128]{1,0:T(8,128)(2,1)}, f32[1,96]{1,0:T(1,128)}, f32[1,96]{1,0:T(1,128)}, bf16[96,16384]{1,0:T(8,128)(2,1)}, /*index=5*/f32[1,1024]{1,0:T(1,128)}) custom-call(bf16[1024,128]{1,0:T(8,128)(2,1)} %acts_hbm.1, s32[96,128]{1,0:T(8,128)} %mask_hbm.1, f32[1,96]{1,0:T(1,128)} %bitcast.7, ...), custom_call_target="tpu_custom_call" | custom-call | tf_op jit(solution)/shard_map/crosscoder/pallas_call | solution.py:554
  81.1 7.4 %last_products.1 = (bf16[96,16384]{1,0:T(8,128)(2,1)}, bf16[96,16384]{1,0:T(8,128)(2,1)}, f32[1,96]{1,0:T(1,128)}, f32[1,96]{1,0:T(1,128)}, f32[1,1024]{1,0:T(1,128)}) custom-call(bf16[16,128,1024]{2,1,0:T(8,128)(2,1)} %get-tuple-element.16.acts_in, bf16[96,128]{1,0:T(8,128)(2,1)} %get-tuple-element.17.gpre_ref, bf16[96,16384]{1,0:T(8,128)(2,1)} %get-tuple-element.18.gd_in, ...), custom_call_target="tpu_custom_call" | custom-call | tf_op jit(solution)/shard_map/last_products/pallas_call | solution.py:604
